TPU v7x, 256 devices: a whole 4x4x8 slice. The times are simulated.
256 devices in a mesh: vec: 4 (over x_hi, core), grid: 64 (over y, z, x_lo).
Axes of the slice: x: 4 (x_hi: 2, x_lo: 2; x = x_hi * 2 + x_lo), y: 4, z: 8, core: 2. Of those that a mesh axis runs over, the one named last changes fastest.
Arguments:
- start_block: float32 [16, 256, 192, 256], P('vec', 'grid'), may hold values from -10 to 10
- potential: float32 [256, 192, 256], P('grid'), may hold values from 0.2 to 1.5
Outputs:
- rotated: float32 [16, 256, 192, 256], P('vec', 'grid')
- rotated_image: float32 [16, 256, 192, 256], P('vec', 'grid')
- ritz_block: float32 [16, 16], replicated
All inputs are finite; a program needn't handle non-finite values.
Results may differ from a plain program's by a relative error of at most 0.00014.
Values sent between devices are 32-bit elements; how exact they have to be, the bound alone decides.
A program may use at most 128 MiB of HBM per device.

v0:
```python
import jax
import jax.numpy as jnp
from jax import lax
from jax.sharding import PartitionSpec as P

AXIAL_COEF = 0.25
CROSS_COEF = 0.25
FILTER_MID = 3.0
FILTER_HALF = 2.0


def extended(x, sides, width):
    for axis, dim in sides:
        count, length = (lax.axis_size(axis), x.shape[dim])
        up = [(i, (i + 1) % count) for i in range(count)]
        down = [(j, i) for i, j in up]
        last = lax.slice_in_dim(x, length - width, length, axis=dim)
        first = lax.slice_in_dim(x, 0, width, axis=dim)
        before = lax.ppermute(last, axis, up)
        after = lax.ppermute(first, axis, down)
        x = jnp.concatenate([before, x, after], axis=dim)
    return x


def op_ext(padded, coef_mid):
    center_planes = padded[..., 2:-2, :, :]
    axial = AXIAL_COEF * (
        2.5 * center_planes
        - 4.0 / 3.0 * (padded[..., 1:-3, :, :] + padded[..., 3:-1, :, :])
        + 1.0 / 12.0 * (padded[..., 0:-4, :, :] + padded[..., 4:, :, :])
    )
    pad_side = [(0, 0)] * (center_planes.ndim - 2)
    along_y = jnp.pad(center_planes, pad_side + [(1, 1), (0, 0)])
    along_z = jnp.pad(center_planes, pad_side + [(0, 0), (1, 1)])
    cross_y = CROSS_COEF * (2.0 * center_planes - along_y[..., :-2, :] - along_y[..., 2:, :])
    cross_z = CROSS_COEF * (2.0 * center_planes - along_z[..., :-2] - along_z[..., 2:])
    return axial + cross_y + cross_z + coef_mid * center_planes


def inner_rows(left_rows, right_rows):
    return lax.dot_general(
        left_rows,
        right_rows,
        (((1,), (1,)), ((), ())),
        precision=lax.Precision.HIGHEST,
        preferred_element_type=jnp.float32,
    )


def body(start_block, potential):
    vec_count = start_block.shape[0]
    groups = lax.axis_size("vec")
    total_vecs = vec_count * groups
    start_ext = extended(start_block, (("grid", 1),), 2)
    first_pass = (op_ext(start_ext, potential) - FILTER_MID * start_block) / FILTER_HALF
    first_ext = extended(first_pass, (("grid", 1),), 2)
    second_pass = (
        2.0 * (op_ext(first_ext, potential) - FILTER_MID * first_pass) / FILTER_HALF - start_block
    )
    second_ext = extended(second_pass, (("grid", 1),), 2)
    applied = op_ext(second_ext, potential)
    flat_block = second_pass.reshape(vec_count, -1)
    flat_applied = applied.reshape(vec_count, -1)
    gathered, gathered_image = (
        lax.all_gather(flat_block, "vec", axis=0, tiled=True),
        lax.all_gather(flat_applied, "vec", axis=0, tiled=True),
    )
    gram_cols = inner_rows(gathered, flat_block)
    curv_cols = inner_rows(gathered, flat_applied)
    gram_sum, curv_sum = lax.psum((gram_cols, curv_cols), "grid")
    gram, curvature = (
        lax.all_gather(gram_sum, "vec", axis=1, tiled=True),
        lax.all_gather(curv_sum, "vec", axis=1, tiled=True),
    )
    factor = jnp.linalg.cholesky(gram)
    inverse = jax.scipy.linalg.solve_triangular(
        factor, jnp.eye(total_vecs, dtype=jnp.float32), lower=True
    )
    ritz_block = jnp.dot(
        jnp.dot(inverse, curvature, precision=lax.Precision.HIGHEST),
        inverse.T,
        precision=lax.Precision.HIGHEST,
    )
    mine_rows = lax.dynamic_slice_in_dim(inverse, lax.axis_index("vec") * vec_count, vec_count, 0)
    combined = jnp.dot(mine_rows, gathered, precision=lax.Precision.HIGHEST)
    combined_image = jnp.dot(mine_rows, gathered_image, precision=lax.Precision.HIGHEST)
    norm_scale = jnp.sqrt(jnp.float32(flat_block.shape[1] * lax.axis_size("grid")))
    rotated = (combined * norm_scale).reshape(second_pass.shape)
    rotated_image = (combined_image * norm_scale).reshape(second_pass.shape)
    return (rotated, rotated_image, ritz_block)


def solution(mesh):
    in_specs = (P("vec", "grid", None, None), P("grid", None, None))
    out_specs = (P("vec", "grid", None, None), P("vec", "grid", None, None), P())
    return jax.shard_map(body, mesh=mesh, in_specs=in_specs, out_specs=out_specs, check_vma=False)
```

profile of v0, /device:TPU:1, one launch (start us, length us, event | category | flops | bytes accessed | tf_op | source)
XLA Modules:
  0.0 585.7 jit_solution(12963983269092796616)
XLA Ops:
  7.2 2.2 fusion.57
  9.4 2.1 collective-permute-start
  11.5 7.8 %collective-permute-start.1 = (f32[4,2,192,256]{3,2,1,0:T(8,128)S(1)}, f32[4,2,192,256]{3,2,1,0:T(8,128)S(1)}, u32[]{:S(2)}, u32[]{:S(2)}) collective-permute-start(f32[4,2,192,256]{3,2,1,0:T(8,128)S(1)} %get-tuple-element.14), channel_id=1, source_target_pairs={{1,0},{2,1},{3,2},{4,3},{5,4},{6,5},{7,6},{8,7},{9,8},{10,9},{11,1... | collective-permute-start | bytes 4718600 | tf_op jit(solution)/shard_map/ppermute | solution.py:20
  19.4 58.7 %collective-permute-done = f32[4,2,192,256]{3,2,1,0:T(8,128)S(1)} collective-permute-done((f32[4,2,192,256]{3,2,1,0:T(8,128)S(1)}, f32[4,2,192,256]{3,2,1,0:T(8,128)S(1)}, u32[]{:S(2)}, u32[]{:S(2)}) %collective-permute-start) | collective-permute-done | bytes 1572896 | tf_op jit(solution)/shard_map/ppermute | solution.py:19
  78.7 1.4 collective-permute-done.1
  80.8 6.4 %broadcast_multiply_fusion = (f32[4,4,192,256]{3,2,1,0:T(8,128)S(1)}, f32[4,4,192,256]{3,2,1,0:T(8,128)}) fusion(f32[4,4,192,256]{3,2,1,0:T(8,128)S(1)} %copy-done.1, f32[4,192,256]{2,1,0:T(8,128)S(1)} %copy-done.6, f32[4,6,192,256]{3,2,1,0:T(8,128)S(1)} %constant_dynamic-update-slice_fusion.2, f32[4,6,192,256]{3,2,1,0:T(8,128)} %copy-done.3), kind=kLoop, calls=%fused_computation.75 | loop fusion | flops 15728640 | bytes 22806528 | tf_op jit(solution)/shard_map/div | solution.py:55
  87.5 10.3 %collective-permute-start.3 = (f32[4,2,192,256]{3,2,1,0:T(8,128)S(1)}, f32[4,2,192,256]{3,2,1,0:T(8,128)S(1)}, u32[]{:S(2)}, u32[]{:S(2)}) collective-permute-start(f32[4,2,192,256]{3,2,1,0:T(8,128)S(1)} %get-tuple-element.10), channel_id=1, source_target_pairs={{1,0},{2,1},{3,2},{4,3},{5,4},{6,5},{7,6},{8,7},{9,8},{10,9},{11,1... | collective-permute-start | bytes 4718600 | tf_op jit(solution)/shard_map/ppermute | solution.py:20
  98.7 57.6 %collective-permute-done.3 = f32[4,2,192,256]{3,2,1,0:T(8,128)S(1)} collective-permute-done((f32[4,2,192,256]{3,2,1,0:T(8,128)S(1)}, f32[4,2,192,256]{3,2,1,0:T(8,128)S(1)}, u32[]{:S(2)}, u32[]{:S(2)}) %collective-permute-start.3) | collective-permute-done | bytes 1572896 | tf_op jit(solution)/shard_map/ppermute | solution.py:20
  156.3 2.1 collective-permute-done.2
  159.6 6.4 %fusion.14 = f32[4,4,192,256]{3,2,1,0:T(8,128)S(1)} fusion(f32[4,4,192,256]{3,2,1,0:T(8,128)S(1)} %copy-done.1, f32[4,4,192,256]{3,2,1,0:T(8,128)} %get-tuple-element.6, f32[4,4,192,256]{3,2,1,0:T(8,128)S(1)} %get-tuple-element.5, f32[4,2,192,256]{3,2,1,0:T(8,128)} %copy-done.8, f32[4,2,192,256]{3,2,1,0:T(8,128)} %copy-done.9, ...), kind=kLoop, calls=%fused_computation.36 | loop fusion | flops 18087936 | bytes 16515072 | tf_op jit(solution)/shard_map/sub | solution.py:58
  166.1 3.2 reshape.33
  169.7 7.9 %collective-permute-start.5 = (f32[4,2,192,256]{3,2,1,0:T(8,128)S(1)}, f32[4,2,192,256]{3,2,1,0:T(8,128)S(1)}, u32[]{:S(2)}, u32[]{:S(2)}) collective-permute-start(f32[4,2,192,256]{3,2,1,0:T(8,128)S(1)} %get-tuple-element.8), channel_id=1, source_target_pairs={{1,0},{2,1},{3,2},{4,3},{5,4},{6,5},{7,6},{8,7},{9,8},{10,9},{11,1... | collective-permute-start | bytes 4718600 | tf_op jit(solution)/shard_map/ppermute | solution.py:20
  178.1 85.6 %collective-permute-done.5 = f32[4,2,192,256]{3,2,1,0:T(8,128)S(1)} collective-permute-done((f32[4,2,192,256]{3,2,1,0:T(8,128)S(1)}, f32[4,2,192,256]{3,2,1,0:T(8,128)S(1)}, u32[]{:S(2)}, u32[]{:S(2)}) %collective-permute-start.5) | collective-permute-done | bytes 1572896 | tf_op jit(solution)/shard_map/ppermute | solution.py:20
  263.7 10.5 %collective-permute-done.4 = f32[4,2,192,256]{3,2,1,0:T(8,128)S(1)} collective-permute-done((f32[4,2,192,256]{3,2,1,0:T(8,128)S(1)}, f32[4,2,192,256]{3,2,1,0:T(8,128)S(1)}, u32[]{:S(2)}, u32[]{:S(2)}) %collective-permute-start.4) | collective-permute-done | bytes 1572896 | tf_op jit(solution)/shard_map/ppermute | solution.py:19
  274.2 5.1 fusion.20
  279.3 5.1 reshape.37
  284.4 3.7 copy.7
  288.1 3.7 copy.10
  291.8 22.0 %all-gather.7.cloned.1.call-done = f32[4,4,196608]{2,1,0:T(4,128)} async-done(((f32[1,4,196608]{2,1,0:T(4,128)}), f32[4,4,196608]{2,1,0:T(4,128)}) %all-gather.7.cloned.1.call-update) | async-done | bytes 12582928 | tf_op jit(solution)/shard_map/all_gather | solution.py:65
  313.8 15.8 %reshape.34 = f32[16,196608]{1,0:T(8,128)} reshape(f32[4,4,196608]{2,1,0:T(4,128)} %all-gather.7.cloned.1.call-done) | data formatting | bytes 25165824
  329.6 18.3 %fusion.58 = f32[16,4]{0,1:T(4,128)S(1)} fusion(f32[16,196608]{1,0:T(8,128)} %reshape.34, f32[4,196608]{1,0:T(4,128)S(1)} %bitcast.45), kind=kOutput, calls=%fused_computation.97 | convolution fusion | flops 150994944 | bytes 15728896 | tf_op jit(solution)/shard_map/dot_general | solution.py:41
  348.0 15.1 %fusion.59 = f32[16,4]{0,1:T(4,128)S(1)} fusion(f32[16,196608]{1,0:T(8,128)S(1)} %copy-done, f32[4,196608]{1,0:T(4,128)S(1)} %bitcast.46), kind=kOutput, calls=%fused_computation.98 | convolution fusion | flops 150994944 | bytes 15728896 | tf_op jit(solution)/shard_map/dot_general | solution.py:41
  363.1 130.6 %all-reduce.6 = (f32[16,4]{0,1:T(4,128)S(1)}, f32[16,4]{0,1:T(4,128)S(1)}) all-reduce(f32[16,4]{0,1:T(4,128)S(1)} %fusion.58, f32[16,4]{0,1:T(4,128)S(1)} %fusion.59), channel_id=1, replica_groups=mesh['vec'=4,'grid'=64] {'grid'}, use_global_device_ids=true, to_apply=%region_0.1 | all-reduce | flops 128 | bytes 1024 | tf_op jit(solution)/shard_map/psum | solution.py:70
  493.7 34.4 %all-gather.1 = f32[4,4,16]{2,1,0:T(4,128)S(1)} all-gather(f32[1,4,16]{2,1,0:T(4,128)S(1)} %bitcast.53), channel_id=1, replica_groups=mesh['vec'=4,'grid'=64] {'vec'}, dimensions={0}, use_global_device_ids=true | all-gather | bytes 1280 | tf_op jit(solution)/shard_map/all_gather | solution.py:72
  528.1 1.5 cholesky.17
  530.9 1.2 custom-call.7
  532.3 9.5 %convolution_multiply_fusion.1 = f32[4,196608]{1,0:T(4,128)S(1)} fusion(f32[16,196608]{1,0:T(8,128)} %reshape.34, f32[16,16]{1,0:T(8,128)S(1)} %fusion.48, s32[]{:T(128)S(6)} %select_n.8), kind=kOutput, calls=%fused_computation.1 | convolution fusion | flops 151781376 | bytes 15730692 | tf_op jit(solution)/shard_map/dot_general | solution.py:85
  541.8 2.2 copy.8
  544.1 6.7 %all-gather.3 = f32[4,4,16]{2,1,0:T(4,128)S(1)} all-gather(f32[1,4,16]{2,1,0:T(4,128)S(1)} %bitcast.52), channel_id=1, replica_groups=mesh['vec'=4,'grid'=64] {'vec'}, dimensions={0}, use_global_device_ids=true | all-gather | bytes 1280 | tf_op jit(solution)/shard_map/all_gather | solution.py:73
  551.6 15.3 %reshape.38 = f32[16,196608]{1,0:T(8,128)} reshape(f32[4,4,196608]{2,1,0:T(4,128)} %all-gather.9.cloned.1.call-done) | data formatting | bytes 25165824
  566.9 9.5 %convolution_multiply_fusion = f32[4,196608]{1,0:T(4,128)S(1)} fusion(f32[16,196608]{1,0:T(8,128)} %reshape.38, f32[16,16]{1,0:T(8,128)S(1)} %fusion.48, s32[]{:T(128)S(6)} %select_n.8), kind=kOutput, calls=%fused_computation | convolution fusion | flops 151781376 | bytes 15730692 | tf_op jit(solution)/shard_map/dot_general | solution.py:86
  576.4 2.2 copy.9
  (41 shorter events, 7.1 us)
Async XLA Ops:
  7.2 306.6 %all-gather.7.cloned.1.call-start = ((), (), s32[]{:S(2)}) async-start(), calls=%async_computation | async-start | bytes 15728640 | tf_op jit(solution)/shard_map/all_gather | solution.py:65
  9.4 68.8 %copy-start.1 = (f32[4,4,192,256]{3,2,1,0:T(8,128)S(1)}, f32[4,4,192,256]{3,2,1,0:T(8,128)}, u32[]{:S(2)}) copy-start(f32[4,4,192,256]{3,2,1,0:T(8,128)} %param.2) | copy-start | bytes 9437188
  9.4 68.6 %collective-permute-start = (f32[4,2,192,256]{3,2,1,0:T(8,128)S(1)}, f32[4,2,192,256]{3,2,1,0:T(8,128)S(1)}, u32[]{:S(2)}, u32[]{:S(2)}) collective-permute-start(f32[4,2,192,256]{3,2,1,0:T(8,128)S(1)} %get-tuple-element.13), channel_id=1, source_target_pairs={{0,1},{1,2},{2,3},{3,4},{4,5},{5,6},{6,7},{7,8},{8,9},{9,10},{10,1... | collective-permute-start | bytes 4718600 | tf_op jit(solution)/shard_map/ppermute | solution.py:19
  11.5 68.6 %collective-permute-start.1 = (f32[4,2,192,256]{3,2,1,0:T(8,128)S(1)}, f32[4,2,192,256]{3,2,1,0:T(8,128)S(1)}, u32[]{:S(2)}, u32[]{:S(2)}) collective-permute-start(f32[4,2,192,256]{3,2,1,0:T(8,128)S(1)} %get-tuple-element.14), channel_id=1, source_target_pairs={{1,0},{2,1},{3,2},{4,3},{5,4},{6,5},{7,6},{8,7},{9,8},{10,9},{11,1... | collective-permute-start | bytes 4718600 | tf_op jit(solution)/shard_map/ppermute | solution.py:20
  78.7 2.1 copy-start.3
  78.7 2.1 copy-start.6
  87.5 68.9 %collective-permute-start.3 = (f32[4,2,192,256]{3,2,1,0:T(8,128)S(1)}, f32[4,2,192,256]{3,2,1,0:T(8,128)S(1)}, u32[]{:S(2)}, u32[]{:S(2)}) collective-permute-start(f32[4,2,192,256]{3,2,1,0:T(8,128)S(1)} %get-tuple-element.10), channel_id=1, source_target_pairs={{1,0},{2,1},{3,2},{4,3},{5,4},{6,5},{7,6},{8,7},{9,8},{10,9},{11,1... | collective-permute-start | bytes 4718600 | tf_op jit(solution)/shard_map/ppermute | solution.py:20
  97.8 60.7 %collective-permute-start.2 = (f32[4,2,192,256]{3,2,1,0:T(8,128)S(1)}, f32[4,2,192,256]{3,2,1,0:T(8,128)S(1)}, u32[]{:S(2)}, u32[]{:S(2)}) collective-permute-start(f32[4,2,192,256]{3,2,1,0:T(8,128)S(1)} %get-tuple-element.9), channel_id=1, source_target_pairs={{0,1},{1,2},{2,3},{3,4},{4,5},{5,6},{6,7},{7,8},{8,9},{9,10},{10,1... | collective-permute-start | bytes 4718600 | tf_op jit(solution)/shard_map/ppermute | solution.py:19
  156.3 2.1 copy-start.8
  158.5 1.2 copy-start.9
  169.3 382.3 %all-gather.9.cloned.1.call-start = ((), (), s32[]{:S(2)}) async-start(), calls=%async_computation.1 | async-start | bytes 15728640 | tf_op jit(solution)/shard_map/all_gather | solution.py:66
  169.4 104.8 %copy-start.7 = (f32[4,192,256]{2,1,0:T(8,128)S(1)}, f32[4,192,256]{2,1,0:T(8,128)}, u32[]{:S(2)}) copy-start(f32[4,192,256]{2,1,0:T(8,128)} %param.3) | copy-start | bytes 2359300
  169.7 94.0 %collective-permute-start.5 = (f32[4,2,192,256]{3,2,1,0:T(8,128)S(1)}, f32[4,2,192,256]{3,2,1,0:T(8,128)S(1)}, u32[]{:S(2)}, u32[]{:S(2)}) collective-permute-start(f32[4,2,192,256]{3,2,1,0:T(8,128)S(1)} %get-tuple-element.8), channel_id=1, source_target_pairs={{1,0},{2,1},{3,2},{4,3},{5,4},{6,5},{7,6},{8,7},{9,8},{10,9},{11,1... | collective-permute-start | bytes 4718600 | tf_op jit(solution)/shard_map/ppermute | solution.py:20
  177.7 96.6 %collective-permute-start.4 = (f32[4,2,192,256]{3,2,1,0:T(8,128)S(1)}, f32[4,2,192,256]{3,2,1,0:T(8,128)S(1)}, u32[]{:S(2)}, u32[]{:S(2)}) collective-permute-start(f32[4,2,192,256]{3,2,1,0:T(8,128)S(1)} %get-tuple-element.7), channel_id=1, source_target_pairs={{0,1},{1,2},{2,3},{3,4},{4,5},{5,6},{6,7},{7,8},{8,9},{9,10},{10,1... | collective-permute-start | bytes 4718600 | tf_op jit(solution)/shard_map/ppermute | solution.py:19
  284.4 3.7 copy-start.2
  291.8 37.8 %copy-start.4 = (f32[1,4,768,256]{3,1,2,0:T(4,128)S(1)}, f32[1,4,768,256]{3,1,2,0:T(4,128)}, u32[]{:S(2)}) copy-start(f32[1,4,768,256]{3,1,2,0:T(4,128)} %copy.7) | copy-start | bytes 9437188
  329.6 18.4 %copy-start = (f32[16,196608]{1,0:T(8,128)S(1)}, f32[16,196608]{1,0:T(8,128)}, u32[]{:S(2)}) copy-start(f32[16,196608]{1,0:T(8,128)} %reshape.34) | copy-start | bytes 37748740
  329.6 18.4 %copy-start.5 = (f32[1,4,768,256]{3,1,2,0:T(4,128)S(1)}, f32[1,4,768,256]{3,1,2,0:T(4,128)}, u32[]{:S(2)}) copy-start(f32[1,4,768,256]{3,1,2,0:T(4,128)} %copy.10) | copy-start | bytes 9437188
Sparse Core Ops, SparseCore 0:
  169.4 144.3 all-gather.6
  315.6 89.0 all-gather.8
where the time goes:
time: 594 us; the launch traced here: 586 us
  waiting for transfers between devices  238 us (40%)
  blocking collectives  172 us (29%)
  local copies, waits for them, and re-layouts  56.6 us (10%)
  matrix products  53.6 us (9%)
  starting transfers between devices  28.7 us (5%)
  other arithmetic  22.9 us (4%)
  between operations  14.4 us (2%)
    ppermute x3, waiting for transfers between devices, extended(): after = lax.ppermute(first, axis, down)  145 us
    psum x1, blocking collectives, body(): gram_sum, curv_sum = lax.psum((gram_cols, curv_cols), 'grid')  131 us
    ppermute x3, waiting for transfers between devices, extended(): before = lax.ppermute(last, axis, up)  71.3 us
    unnamed x30, local copies, waits for them, and re-layouts  53.3 us
    all_gather x1, blocking collectives, body(): lax.all_gather(gram_sum, 'vec', axis=1, tiled=True)  34.4 us
    dot_general x2, matrix products, inner_rows(): lax.dot_general(left_rows, right_rows, (((1,), (1,)), ((), ())), precisio...  33.5 us
    ppermute x3, starting transfers between devices, extended(): after = lax.ppermute(first, axis, down)  26.1 us
    all_gather x1, waiting for transfers between devices, body(): lax.all_gather(flat_block, 'vec', axis=0, tiled=True)  22 us
  transfers between devices with their start and end apart: 8, of which 7 were waited for; matrix products, arithmetic and copies ran while one was open for 15% of the time, Pallas kernels for 0%

commit v1 on v0

v1 whole, which is shorter than its diff:
```python
import functools

import jax
import jax.numpy as jnp
from jax import lax
from jax.experimental import pallas as pl
from jax.experimental.pallas import tpu as pltpu
from jax.sharding import PartitionSpec as P

MESH = pl.DeviceIdType.MESH
F32 = jnp.float32
HI = lax.Precision.HIGHEST
NX, NY, NZ = 4, 4, 8
VPG, GROUPS = 4, 4
PLANES = 4
ROWS = 48
LANES = 256
TOP, BOT = 8, 8 + ROWS
STEP = 16
NT = (((1,), (1,)), ((), ()))


def place():
    vec, grid = lax.axis_index("vec"), lax.axis_index("grid")
    return (vec // 2) * 2 + grid % 2, grid // (2 * NZ), (grid // 2) % NZ, vec % 2


def device(x, y, z, core):
    return ((x // 2) * 2 + core, (y * NZ + z) * 2 + x % 2)


def stencil(src, pot, i, g, p, row, scale, middle):
    rows = pl.ds(row, STEP)
    at = lambda q, r: src[i, g, q, pl.ds(r, STEP), :]
    center = at(p + 2, row)
    lane = lax.broadcasted_iota(jnp.int32, (STEP, LANES), 1)
    left = jnp.where(lane == 0, 0.0, pltpu.roll(center, 1, 1))
    right = jnp.where(lane == LANES - 1, 0.0, pltpu.roll(center, LANES - 1, 1))
    cross = (at(p + 2, row - 1) + at(p + 2, row + 1)) + (left + right)
    near = at(p + 1, row) + at(p + 3, row)
    far = at(p, row) + at(p + 4, row)
    diag = scale * pot[p, pl.ds(row - TOP, STEP), :] + scale * (1.625 - middle)
    return diag * center - (scale / 3.0) * near + (scale / 48.0) * far - (scale * 0.25) * cross


def kernel(start, pot, rot_out, img_out, ritz_out,
           xs, fs, ss, aa, rr, ii, pw, ysend, yrecv, gp, red, mat, inv_s,
           a_send, a_recv, p_send, p_recv, h_send, h_recv, y_send, y_recv,
           r_send, r_recv, o_send, o_recv, s_sem):
    x, y, z, c = place()
    x_lo = x % 2
    mine = lax.axis_index("vec")
    k = y * NZ + z
    ring = NY * NZ

    def at_ring(kk, core):
        kk = (kk + ring) % ring
        return device(x, kk // NZ, kk % NZ, core)

    right = at_ring(k + c, 1 - c)
    left = at_ring(k - (1 - c), 1 - c)
    line = [device(((2 * x + c + d) % 8) // 2, y, z, ((2 * x + c + d) % 8) % 2) for d in range(1, 8)]
    z_peers = [device(x, y, (z + d) % NZ, c) for d in range(1, NZ)]
    y_peers = [device(x, (y + d) % NY, z, c) for d in range(1, NY)]
    far = at_ring(k + 2 * c - 1, 1 - c)

    barrier = pltpu.get_barrier_semaphore()
    peers = line + z_peers + y_peers + [far]
    for peer in peers:
        pl.semaphore_signal(barrier, inc=1, device_id=peer, device_id_type=MESH)
    pl.semaphore_wait(barrier, len(peers))

    def remote(src, dst, send, recv, to):
        return pltpu.make_async_remote_copy(
            src_ref=src, dst_ref=dst, send_sem=send, recv_sem=recv, device_id=to, device_id_type=MESH)

    own_rows = pl.ds(TOP, ROWS)

    def pot_local():
        return pltpu.make_async_copy(pot.at[:, pl.ds(pl.multiple_of(ROWS * x, 8), ROWS), :], pw, p_recv)

    pair_x = x + 1 - 2 * x_lo
    pot_remote = remote(pot.at[:, pl.ds(pl.multiple_of(ROWS * pair_x, 8), ROWS), :], pw, p_send, p_recv,
                        device(pair_x, y, z, c))

    @pl.when(c == x_lo)
    def _():
        pot_local().start()
        pot_remote.start()

    def a_copy(i, d):
        to = (x + d) % NX
        src = start.at[i, :, pl.ds(pl.multiple_of(ROWS * to, 8), ROWS), :]
        dst = xs.at[i, mine, 2:2 + PLANES, own_rows, :]
        return src, dst, to

    def a_remote(i, d):
        src, dst, to = a_copy(i, d)
        return remote(src, dst, a_send.at[i, d], a_recv.at[i, mine], device(to, y, z, x_lo))

    @pl.loop(0, VPG)
    def _(i):
        for d in (2, 1, 3):
            a_remote(i, d).start()

        @pl.when(c == x_lo)
        def _():
            src, dst, _ = a_copy(i, 0)
            pltpu.make_async_copy(src, dst, a_recv.at[i, mine]).start()

        @pl.when(c != x_lo)
        def _():
            a_remote(i, 0).start()

    def a_wait(i):
        for g in range(GROUPS):
            dst = xs.at[i, g, 2:2 + PLANES, own_rows, :]
            remote(dst, dst, a_send.at[i, 0], a_recv.at[i, g], right).wait_recv()

    top_keep = jnp.where(x == 0, 0.0, 1.0).astype(F32)
    bot_keep = jnp.where(x == NX - 1, 0.0, 1.0).astype(F32)
    above = device((x + NX - 1) % NX, y, z, c)
    below = device((x + 1) % NX, y, z, c)

    def halo_copies(buf, s, i):
        return (
            remote(buf.at[i, :, PLANES:PLANES + 2, own_rows, :], buf.at[i, :, 0:2, own_rows, :],
                   h_send.at[s, i, 0], h_recv.at[s, i, 0], right),
            remote(buf.at[i, :, 2:4, own_rows, :], buf.at[i, :, PLANES + 2:PLANES + 4, own_rows, :],
                   h_send.at[s, i, 1], h_recv.at[s, i, 1], left),
            remote(ysend.at[s, i, 0], yrecv.at[s, i, 0], y_send.at[s, i, 0], y_recv.at[s, i, 0], below),
            remote(ysend.at[s, i, 1], yrecv.at[s, i, 1], y_send.at[s, i, 1], y_recv.at[s, i, 1], above),
        )

    def halo_start(buf, s, i):
        @pl.loop(0, GROUPS)
        def _(g):
            for p in range(PLANES):
                ysend[s, i, 0, g, pl.ds(p, 1), :] = buf[i, g, p + 2, pl.ds(BOT - 1, 1), :]
                ysend[s, i, 1, g, pl.ds(p, 1), :] = buf[i, g, p + 2, pl.ds(TOP, 1), :]

        for copy in halo_copies(buf, s, i):
            copy.start()

    def halo_wait(buf, s, i):
        for copy in halo_copies(buf, s, i):
            copy.wait_recv()

        @pl.loop(0, GROUPS)
        def _(g):
            for p in range(PLANES):
                buf[i, g, p + 2, pl.ds(TOP - 1, 1), :] = yrecv[s, i, 0, g, pl.ds(p, 1), :] * top_keep
                buf[i, g, p + 2, pl.ds(BOT, 1), :] = yrecv[s, i, 1, g, pl.ds(p, 1), :] * bot_keep

    def first(i):
        halo_wait(xs, 0, i)

        @pl.loop(0, GROUPS)
        def _(g):
            for p in range(PLANES):
                for row in range(TOP, BOT, STEP):
                    fs[i, g, p + 2, pl.ds(row, STEP), :] = stencil(xs, pw, i, g, p, row, 0.5, 3.0)

        halo_start(fs, 1, i)

    def blocks(i, other, off):
        @pl.loop(0, i + 1)
        def _(j):
            def body(t, accs):
                p, r = t // (ROWS // 8), t % (ROWS // 8)
                row = pl.multiple_of(TOP + 8 * r, 8)
                a = [ss[i, g, p + 2, pl.ds(row, 8), :] for g in range(GROUPS)]
                if off:
                    b = [other[j, h, p, pl.ds(pl.multiple_of(8 * r, 8), 8), :] for h in range(GROUPS)]
                else:
                    b = [other[j, h, p + 2, pl.ds(row, 8), :] for h in range(GROUPS)]
                new = []
                for g in range(GROUPS):
                    for h in range(GROUPS):
                        prod = a[g] * b[h]
                        new.append(accs[g * GROUPS + h] + (prod[:, :128] + prod[:, 128:]))
                return tuple(new)

            zero = jnp.zeros((8, 128), F32)
            accs = lax.fori_loop(0, PLANES * ROWS // 8, body, (zero,) * (GROUPS * GROUPS))
            for g in range(GROUPS):
                for h in range(GROUPS):
                    gp[g * VPG + i, h * VPG + j] = accs[g * GROUPS + h]

            @pl.when(j < i)
            def _():
                for g in range(GROUPS):
                    for h in range(GROUPS):
                        gp[h * VPG + j, g * VPG + i] = accs[g * GROUPS + h]

    def second(i):
        halo_wait(fs, 1, i)

        @pl.loop(0, GROUPS)
        def _(g):
            for p in range(PLANES):
                for row in range(TOP, BOT, STEP):
                    rows = pl.ds(row, STEP)
                    ss[i, g, p + 2, rows, :] = (
                        stencil(fs, pw, i, g, p, row, 1.0, 3.0) - xs[i, g, p + 2, rows, :])

        halo_start(ss, 2, i)
        blocks(i, ss, False)

    def image(i):
        halo_wait(ss, 2, i)

        @pl.loop(0, GROUPS)
        def _(g):
            for p in range(PLANES):
                for row in range(TOP, BOT, STEP):
                    aa[i, g, p, pl.ds(row - TOP, STEP), :] = stencil(ss, pw, i, g, p, row, 1.0, 0.0)

    line_slot = 2 * x + c
    lane16 = lax.broadcasted_iota(jnp.int32, (16, 128), 1)

    def gather_tiles():
        def body(u, out):
            tile = jnp.sum(gp[u], axis=1)
            return jnp.where(lane16 == u, jnp.sum(tile, axis=1, keepdims=True), out)

        return lax.fori_loop(0, 16, body, jnp.zeros((16, 128), F32))

    rounds = ((line, 0, 8, line_slot), (z_peers, 8, NZ, z), (y_peers, 8 + NZ, NY, y))

    def round_copies(w, n):
        to, base, count, own = rounds[n]
        slot = base + own
        return [remote(red.at[w, slot], red.at[w, slot], r_send.at[w, base + d], r_recv.at[w, slot], peer)
                for d, peer in enumerate(to)]

    def round_start(w, n, value):
        to, base, count, own = rounds[n]
        red[w, base + own] = value
        for copy in round_copies(w, n):
            copy.start()

    def round_sum(w, n):
        to, base, count, own = rounds[n]
        for d, peer in enumerate(to):
            slot = base + (own + d + 1) % count
            remote(red.at[w, slot], red.at[w, slot], r_send.at[w, base + d], r_recv.at[w, slot], peer).wait_recv()
        total = red[w, base]
        for q in range(1, count):
            total = total + red[w, base + q]
        return total

    pot_wait = remote(pw, pw, p_send, p_recv, right)

    @pl.loop(0, VPG + 1)
    def _(t):
        @pl.when(t < VPG)
        def _():
            a_wait(t)
            halo_start(xs, 0, t)

        @pl.when(t == 0)
        def _():
            pot_wait.wait_recv()

        @pl.when(t > 0)
        def _():
            second(t - 1)

        @pl.when(t < VPG)
        def _():
            first(t)

    round_start(0, 0, gather_tiles())
    image(0)
    round_start(0, 1, round_sum(0, 0))
    image(1)
    round_start(0, 2, round_sum(0, 1))
    image(2)
    gram = round_sum(0, 2)

    row16 = lax.broadcasted_iota(jnp.int32, (16, 128), 0)
    work = jnp.where(lane16 < 16, gram, jnp.where(lane16 - 16 == row16, 1.0, 0.0))
    for j in range(16):
        scale = 1.0 / jnp.sqrt(work[j:j + 1, j:j + 1])
        pivot = work[j:j + 1, :] * scale
        column = work[:, j:j + 1] * scale
        work = jnp.where(row16 > j, work - column * pivot, jnp.where(row16 == j, pivot, work))
    inverse = jnp.where(lane16 < 16, pltpu.roll(work, 112, 1), 0.0)
    norm = jnp.sqrt(jnp.full((16, 128), PLANES * 64 * ROWS * NX * LANES, F32))
    mat[...] = inverse * norm
    to_smem = pltpu.make_async_copy(mat, inv_s, s_sem)
    to_smem.start()
    to_smem.wait()

    def o_copy(out, buf, w, i, g):
        to_x = 2 * (g // 2) + c
        to_c = g % 2
        dst = out.at[i, :, pl.ds(pl.multiple_of(ROWS * x, 8), ROWS), :]
        here = jnp.logical_and(to_x == x, to_c == c)
        send = remote(buf.at[i, g], dst, o_send.at[w, i, g], o_recv.at[w, i, x], device(to_x, y, z, to_c))
        keep = pltpu.make_async_copy(buf.at[i, g], dst, o_recv.at[w, i, x])
        return here, send, keep

    def rotate(src, lift, buf, out, w):
        @pl.loop(0, VPG * GROUPS)
        def _(n):
            i, g = n // GROUPS, n % GROUPS
            v = g * VPG + i
            coef = [inv_s[v, u] for u in range(16)]

            @pl.loop(0, PLANES)
            def _(p):
                for row in range(0, ROWS, STEP):
                    acc = None
                    for u in range(16):
                        term = coef[u] * src[u % VPG, u // VPG, p + lift, pl.ds(row + (TOP if lift else 0), STEP), :]
                        acc = term if acc is None else acc + term
                    buf[i, g, p, pl.ds(row, STEP), :] = acc

            here, send, keep = o_copy(out, buf, w, i, g)

            @pl.when(here)
            def _():
                keep.start()

            @pl.when(jnp.logical_not(here))
            def _():
                send.start()

    rotate(ss, 2, rr, rot_out, 0)
    image(3)
    rotate(aa, 0, ii, img_out, 1)

    @pl.loop(0, VPG)
    def _(i):
        blocks(i, aa, True)

    round_start(1, 0, gather_tiles())
    round_start(1, 1, round_sum(1, 0))
    round_start(1, 2, round_sum(1, 1))
    curvature = round_sum(1, 2)
    half = lax.dot_general(inverse, curvature, NT, precision=HI, preferred_element_type=F32)
    half = jnp.concatenate([half, jnp.zeros((16, 112), F32)], axis=1)
    ritz_out[...] = lax.dot_general(half, inverse, NT, precision=HI, preferred_element_type=F32)

    @pl.when(c == x_lo)
    def _():
        pot_remote.wait_send()

    @pl.loop(0, VPG)
    def _(i):
        for d in (1, 2, 3):
            a_remote(i, d).wait_send()

        @pl.when(c != x_lo)
        def _():
            a_remote(i, 0).wait_send()

        for s, buf in enumerate((xs, fs, ss)):
            for copy in halo_copies(buf, s, i):
                copy.wait_send()

    for w in range(2):
        for n in range(3):
            for copy in round_copies(w, n):
                copy.wait_send()

    for w, (out, buf) in enumerate(((rot_out, rr), (img_out, ii))):
        @pl.loop(0, VPG * GROUPS)
        def _(n):
            i, g = n // GROUPS, n % GROUPS
            here, send, keep = o_copy(out, buf, w, i, g)

            @pl.when(jnp.logical_not(here))
            def _():
                send.wait_send()

        @pl.loop(0, VPG)
        def _(i):
            for xx in range(NX):
                dst = out.at[i, :, pl.ds(ROWS * xx, ROWS), :]
                remote(dst, dst, o_send.at[w, i, 0], o_recv.at[w, i, xx], right).wait_recv()


def body(start_block, potential):
    dma = pltpu.SemaphoreType.DMA
    any_space = pl.BlockSpec(memory_space=pl.ANY)
    field = pltpu.VMEM((VPG, GROUPS, PLANES + 4, ROWS + 16, LANES), F32)
    inner = pltpu.VMEM((VPG, GROUPS, PLANES, ROWS, LANES), F32)
    return tuple(pl.pallas_call(
        kernel,
        out_shape=(
            jax.ShapeDtypeStruct(start_block.shape, F32),
            jax.ShapeDtypeStruct(start_block.shape, F32),
            jax.ShapeDtypeStruct((16, 16), F32),
        ),
        in_specs=[any_space, any_space],
        out_specs=(any_space, any_space, pl.BlockSpec(memory_space=pltpu.VMEM)),
        scratch_shapes=[
            field, field, field, inner, inner, inner,
            pltpu.VMEM((PLANES, ROWS, LANES), F32),
            pltpu.VMEM((3, VPG, 2, GROUPS, PLANES, LANES), F32),
            pltpu.VMEM((3, VPG, 2, GROUPS, PLANES, LANES), F32),
            pltpu.VMEM((16, 16, 8, 128), F32),
            pltpu.VMEM((2, 8 + NZ + NY, 16, 128), F32),
            pltpu.VMEM((16, 128), F32),
            pltpu.SMEM((16, 128), F32),
            dma((VPG, 4)), dma((VPG, GROUPS)), dma, dma,
            dma((3, VPG, 2)), dma((3, VPG, 2)), dma((3, VPG, 2)), dma((3, VPG, 2)),
            dma((2, 8 + NZ + NY)), dma((2, 8 + NZ + NY)),
            dma((2, VPG, GROUPS)), dma((2, VPG, NX)), dma,
        ],
        compiler_params=pltpu.CompilerParams(
            collective_id=0, has_side_effects=True, vmem_limit_bytes=56 * 2**20),
        name="filtered_subspace",
    )(start_block, potential))


def solution(mesh):
    in_specs = (P("vec", "grid", None, None), P("grid", None, None))
    out_specs = (P("vec", "grid", None, None), P("vec", "grid", None, None), P())
    return jax.shard_map(body, mesh=mesh, in_specs=in_specs, out_specs=out_specs, check_vma=False)
```

time: 594 us -> 204 us (0.34); the launches traced: 586 us -> 203 us
  waiting for transfers between devices: 238 us -> 0 us
  Pallas kernels: 0 us -> 197 us
  blocking collectives: 172 us -> 0 us
  matrix products: 53.6 us -> 0 us
  local copies, waits for them, and re-layouts: 56.6 us -> 6.25 us
  starting transfers between devices: 28.7 us -> 0 us
  other arithmetic: 22.9 us -> 0 us
  between operations: 14.4 us -> 0.65 us
    ppermute x6 -> x0, waiting for transfers between devices: 216 us -> none  [the longest x3 145 us: extended(): after = lax.ppermute(first, axis, down)]
    pallas_call x0 -> x1, Pallas kernels: none -> 197 us  [body(): pl.pallas_call(kernel, out_shape=(jax.ShapeDtypeStruct(start_block.shape,...]
    psum x1 -> x0, blocking collectives: 131 us -> none  [body(): gram_sum, curv_sum = lax.psum((gram_cols, curv_cols), 'grid')]
    dot_general x6 -> x0, matrix products: 53.4 us -> none  [the longest x2 33.5 us: inner_rows(): lax.dot_general(left_rows, right_rows, (((1,), (1,)), ((), ())), precisio...]
    unnamed x30 -> x7, local copies, waits for them, and re-layouts: 53.3 us -> 6.25 us
    all_gather x2 -> x0, blocking collectives: 41 us -> none  [the longest x1 34.4 us: body(): lax.all_gather(gram_sum, 'vec', axis=1, tiled=True)]
    ppermute x6 -> x0, starting transfers between devices: 28.6 us -> none  [the longest x3 26.1 us: extended(): after = lax.ppermute(first, axis, down)]
    all_gather x2 -> x0, waiting for transfers between devices: 22 us -> none  [the longest x1 22 us: body(): lax.all_gather(flat_block, 'vec', axis=0, tiled=True)]
  transfers between devices with their start and end apart: 8 -> 0, of which waited for: 7 -> 0; matrix products, arithmetic and copies ran while one was open for 15% -> 0% of each run, Pallas kernels for 0% -> 0%
where the time goes in v1:
time: 204 us; the launch traced here: 203 us
  Pallas kernels  197 us (97%)
  local copies, waits for them, and re-layouts  6.25 us (3%)
    pallas_call x1, Pallas kernels, body(): pl.pallas_call(kernel, out_shape=(jax.ShapeDtypeStruct(start_block.shape,...  197 us
    unnamed x7, local copies, waits for them, and re-layouts  6.25 us

profile of v1, /device:TPU:1, one launch (start us, length us, event | category | flops | bytes accessed | tf_op | source)
XLA Modules:
  0.0 203.4 jit_solution(1754660593560780475)
XLA Ops:
  0.6 196.5 %filtered_subspace.1 = (f32[4,4,192,256]{3,2,1,0:T(8,128)}, f32[4,4,192,256]{3,2,1,0:T(8,128)}, f32[16,16]{1,0:T(8,128)}) custom-call(f32[4,4,192,256]{3,2,1,0:T(8,128)} %start.1, f32[4,192,256]{2,1,0:T(8,128)} %pot.1), custom_call_target="tpu_custom_call" | custom-call | tf_op jit(solution)/shard_map/filtered_subspace/pallas_call | solution.py:391
  197.2 0.0 copy-start
  197.2 4.0 %copy.8 = f32[4,4,192,256]{3,2,1,0:T(8,128)} copy(f32[4,4,192,256]{3,2,1,0:T(8,128)} %get-tuple-element.6) | data formatting | bytes 6291456
  201.2 0.0 copy-done
  201.2 0.0 copy-start.1
  201.2 1.7 copy.9
  202.8 0.0 copy-done.1
  202.8 0.6 copy.10
Async XLA Ops:
  197.2 4.0 %copy-start = (f32[4,4,192,256]{3,2,1,0:T(8,128)S(1)}, f32[4,4,192,256]{3,2,1,0:T(8,128)}, u32[]{:S(2)}) copy-start(f32[4,4,192,256]{3,2,1,0:T(8,128)} %get-tuple-element.7) | copy-start | bytes 9437188
  201.2 1.7 copy-start.1

commit v2 on v1

--- a/solution.py
+++ b/solution.py
@@ -44,8 +44,8 @@
 
 
 def kernel(start, pot, rot_out, img_out, ritz_out,
-           xs, fs, ss, aa, rr, ii, pw, ysend, yrecv, gp, red, mat, inv_s,
-           a_send, a_recv, p_send, p_recv, h_send, h_recv, y_send, y_recv,
+           xs, fs, ss, aa, rr, ii, pw, edge, pack, xy, ysend, yrecv, gp, red, mat, inv_s,
+           a_send, a_recv, e_sem, k_send, k_recv, p_send, p_recv, h_send, h_recv, y_send, y_recv,
            r_send, r_recv, o_send, o_recv, s_sem):
     x, y, z, c = place()
     x_lo = x % 2
@@ -98,133 +98,205 @@
         src, dst, to = a_copy(i, d)
         return remote(src, dst, a_send.at[i, d], a_recv.at[i, mine], device(to, y, z, x_lo))
 
+    def a_start(i):
+        for d in (2, 1, 3):
+            a_remote(i, d).start()
+
+        @pl.when(c == x_lo)
+        def _():
+            src, dst, _ = a_copy(i, 0)
+            pltpu.make_async_copy(src, dst, a_recv.at[i, mine]).start()
+
+        @pl.when(c != x_lo)
+        def _():
+            a_remote(i, 0).start()
+
+    def e_copy(b):
+        return pltpu.make_async_copy(start.at[:, :, pl.ds(ROWS * (b + 1) - 8, 16), :], edge.at[b], e_sem.at[b])
+
+    def k_remote(d):
+        to = (x + d) % NX
+        return remote(pack.at[to], xy.at[mine], k_send.at[d], k_recv.at[mine], device(to, y, z, x_lo))
+
+    for b in range(NX - 1):
+        e_copy(b).start()
+    a_start(0)
+    for b in range(NX - 1):
+        e_copy(b).wait()
+
     @pl.loop(0, VPG)
     def _(i):
-        for d in (2, 1, 3):
-            a_remote(i, d).start()
-
-        @pl.when(c == x_lo)
-        def _():
-            src, dst, _ = a_copy(i, 0)
-            pltpu.make_async_copy(src, dst, a_recv.at[i, mine]).start()
-
-        @pl.when(c != x_lo)
-        def _():
-            a_remote(i, 0).start()
-
-    def a_wait(i):
-        for g in range(GROUPS):
-            dst = xs.at[i, g, 2:2 + PLANES, own_rows, :]
-            remote(dst, dst, a_send.at[i, 0], a_recv.at[i, g], right).wait_recv()
+        for p in range(PLANES):
+            for q in range(NX):
+                zero = jnp.zeros((1, LANES), F32)
+                above_row = edge[q - 1, i, p, pl.ds(7, 1), :] if q else zero
+                below_row = edge[q, i, p, pl.ds(8, 1), :] if q < NX - 1 else zero
+                pack[q, i, 0, pl.ds(p, 1), :] = above_row
+                pack[q, i, 1, pl.ds(p, 1), :] = below_row
+
+    for d in (2, 1, 3):
+        k_remote(d).start()
+
+    @pl.when(c == x_lo)
+    def _():
+        pltpu.make_async_copy(pack.at[x], xy.at[mine], k_recv.at[mine]).start()
+
+    @pl.when(c != x_lo)
+    def _():
+        k_remote(0).start()
+
+    @pl.loop(1, VPG)
+    def _(i):
+        a_start(i)
+
+    def a_wait(n):
+        i, h = n // 2, n % 2
+        for e in range(2):
+            dst = xs.at[i, 2 * h + e, 2:2 + PLANES, own_rows, :]
+            remote(dst, dst, a_send.at[i, 0], a_recv.at[i, 2 * h + e], right).wait_recv()
 
     top_keep = jnp.where(x == 0, 0.0, 1.0).astype(F32)
     bot_keep = jnp.where(x == NX - 1, 0.0, 1.0).astype(F32)
     above = device((x + NX - 1) % NX, y, z, c)
     below = device((x + 1) % NX, y, z, c)
 
-    def halo_copies(buf, s, i):
+    def plane_copies(buf, s, n):
+        i, gs = n // 2, pl.ds(2 * (n % 2), 2)
         return (
-            remote(buf.at[i, :, PLANES:PLANES + 2, own_rows, :], buf.at[i, :, 0:2, own_rows, :],
-                   h_send.at[s, i, 0], h_recv.at[s, i, 0], right),
-            remote(buf.at[i, :, 2:4, own_rows, :], buf.at[i, :, PLANES + 2:PLANES + 4, own_rows, :],
-                   h_send.at[s, i, 1], h_recv.at[s, i, 1], left),
-            remote(ysend.at[s, i, 0], yrecv.at[s, i, 0], y_send.at[s, i, 0], y_recv.at[s, i, 0], below),
-            remote(ysend.at[s, i, 1], yrecv.at[s, i, 1], y_send.at[s, i, 1], y_recv.at[s, i, 1], above),
+            remote(buf.at[i, gs, PLANES:PLANES + 2, own_rows, :], buf.at[i, gs, 0:2, own_rows, :],
+                   h_send.at[s, n, 0], h_recv.at[s, n, 0], right),
+            remote(buf.at[i, gs, 2:4, own_rows, :], buf.at[i, gs, PLANES + 2:PLANES + 4, own_rows, :],
+                   h_send.at[s, n, 1], h_recv.at[s, n, 1], left),
         )
 
-    def halo_start(buf, s, i):
-        @pl.loop(0, GROUPS)
-        def _(g):
+    def row_copies(s, n):
+        return (
+            remote(ysend.at[s, n, 0], yrecv.at[s, n, 0], y_send.at[s, n, 0], y_recv.at[s, n, 0], below),
+            remote(ysend.at[s, n, 1], yrecv.at[s, n, 1], y_send.at[s, n, 1], y_recv.at[s, n, 1], above),
+        )
+
+    def row_start(buf, s, n):
+        i, h = n // 2, n % 2
+        for e in range(2):
             for p in range(PLANES):
-                ysend[s, i, 0, g, pl.ds(p, 1), :] = buf[i, g, p + 2, pl.ds(BOT - 1, 1), :]
-                ysend[s, i, 1, g, pl.ds(p, 1), :] = buf[i, g, p + 2, pl.ds(TOP, 1), :]
-
-        for copy in halo_copies(buf, s, i):
+                ysend[s, n, 0, e, pl.ds(p, 1), :] = buf[i, 2 * h + e, p + 2, pl.ds(BOT - 1, 1), :]
+                ysend[s, n, 1, e, pl.ds(p, 1), :] = buf[i, 2 * h + e, p + 2, pl.ds(TOP, 1), :]
+
+        for copy in row_copies(s, n):
             copy.start()
 
-    def halo_wait(buf, s, i):
-        for copy in halo_copies(buf, s, i):
+    def plane_start(buf, s, n):
+        for copy in plane_copies(buf, s, n):
+            copy.start()
+
+    def plane_wait(buf, s, n):
+        for copy in plane_copies(buf, s, n):
             copy.wait_recv()
 
-        @pl.loop(0, GROUPS)
-        def _(g):
+    def row_wait(buf, s, n):
+        i, h = n // 2, n % 2
+        for copy in row_copies(s, n):
+            copy.wait_recv()
+
+        for e in range(2):
             for p in range(PLANES):
-                buf[i, g, p + 2, pl.ds(TOP - 1, 1), :] = yrecv[s, i, 0, g, pl.ds(p, 1), :] * top_keep
-                buf[i, g, p + 2, pl.ds(BOT, 1), :] = yrecv[s, i, 1, g, pl.ds(p, 1), :] * bot_keep
-
-    def first(i):
-        halo_wait(xs, 0, i)
-
-        @pl.loop(0, GROUPS)
-        def _(g):
+                buf[i, 2 * h + e, p + 2, pl.ds(TOP - 1, 1), :] = yrecv[s, n, 0, e, pl.ds(p, 1), :] * top_keep
+                buf[i, 2 * h + e, p + 2, pl.ds(BOT, 1), :] = yrecv[s, n, 1, e, pl.ds(p, 1), :] * bot_keep
+
+    def first(n):
+        i = n // 2
+        plane_wait(xs, 0, n)
+
+        @pl.loop(0, 2)
+        def _(e):
+            g = 2 * (n % 2) + e
+            for p in range(PLANES):
+                xs[i, g, p + 2, pl.ds(TOP - 1, 1), :] = xy[g, i, 0, pl.ds(p, 1), :]
+                xs[i, g, p + 2, pl.ds(BOT, 1), :] = xy[g, i, 1, pl.ds(p, 1), :]
             for p in range(PLANES):
                 for row in range(TOP, BOT, STEP):
                     fs[i, g, p + 2, pl.ds(row, STEP), :] = stencil(xs, pw, i, g, p, row, 0.5, 3.0)
 
-        halo_start(fs, 1, i)
-
-    def blocks(i, other, off):
-        @pl.loop(0, i + 1)
+        plane_start(fs, 1, n)
+        row_start(fs, 0, n)
+
+    def block(i, gs, j, other, off):
+        def step(t, accs):
+            p, r = t // (ROWS // 8), t % (ROWS // 8)
+            row = pl.multiple_of(TOP + 8 * r, 8)
+            a = [ss[i, g, p + 2, pl.ds(row, 8), :] for g in gs]
+            if off:
+                b = [other[j, h, p, pl.ds(pl.multiple_of(8 * r, 8), 8), :] for h in range(GROUPS)]
+            else:
+                b = [other[j, h, p + 2, pl.ds(row, 8), :] for h in range(GROUPS)]
+            new = []
+            for q in range(len(gs)):
+                for h in range(GROUPS):
+                    prod = a[q] * b[h]
+                    new.append(accs[q * GROUPS + h] + (prod[:, :128] + prod[:, 128:]))
+            return tuple(new)
+
+        zero = jnp.zeros((8, 128), F32)
+        return lax.fori_loop(0, PLANES * ROWS // 8, step, (zero,) * (len(gs) * GROUPS))
+
+    def blocks(n, other, off):
+        i, h = n // 2, n % 2
+
+        @pl.loop(0, i)
         def _(j):
-            def body(t, accs):
-                p, r = t // (ROWS // 8), t % (ROWS // 8)
-                row = pl.multiple_of(TOP + 8 * r, 8)
-                a = [ss[i, g, p + 2, pl.ds(row, 8), :] for g in range(GROUPS)]
-                if off:
-                    b = [other[j, h, p, pl.ds(pl.multiple_of(8 * r, 8), 8), :] for h in range(GROUPS)]
-                else:
-                    b = [other[j, h, p + 2, pl.ds(row, 8), :] for h in range(GROUPS)]
-                new = []
-                for g in range(GROUPS):
-                    for h in range(GROUPS):
-                        prod = a[g] * b[h]
-                        new.append(accs[g * GROUPS + h] + (prod[:, :128] + prod[:, 128:]))
-                return tuple(new)
-
-            zero = jnp.zeros((8, 128), F32)
-            accs = lax.fori_loop(0, PLANES * ROWS // 8, body, (zero,) * (GROUPS * GROUPS))
+            gs = (2 * h, 2 * h + 1)
+            accs = block(i, gs, j, other, off)
+            for q, g in enumerate(gs):
+                for o in range(GROUPS):
+                    gp[g * VPG + i, o * VPG + j] = accs[q * GROUPS + o]
+                    gp[o * VPG + j, g * VPG + i] = accs[q * GROUPS + o]
+
+        @pl.when(h == 1)
+        def _():
+            accs = block(i, range(GROUPS), i, other, off)
             for g in range(GROUPS):
-                for h in range(GROUPS):
-                    gp[g * VPG + i, h * VPG + j] = accs[g * GROUPS + h]
-
-            @pl.when(j < i)
-            def _():
-                for g in range(GROUPS):
-                    for h in range(GROUPS):
-                        gp[h * VPG + j, g * VPG + i] = accs[g * GROUPS + h]
-
-    def second(i):
-        halo_wait(fs, 1, i)
-
-        @pl.loop(0, GROUPS)
-        def _(g):
+                for o in range(GROUPS):
+                    gp[g * VPG + i, o * VPG + i] = accs[g * GROUPS + o]
+
+    def second(n):
+        i = n // 2
+        plane_wait(fs, 1, n)
+        row_wait(fs, 0, n)
+
+        @pl.loop(0, 2)
+        def _(e):
+            g = 2 * (n % 2) + e
             for p in range(PLANES):
                 for row in range(TOP, BOT, STEP):
                     rows = pl.ds(row, STEP)
                     ss[i, g, p + 2, rows, :] = (
                         stencil(fs, pw, i, g, p, row, 1.0, 3.0) - xs[i, g, p + 2, rows, :])
 
-        halo_start(ss, 2, i)
-        blocks(i, ss, False)
-
-    def image(i):
-        halo_wait(ss, 2, i)
-
-        @pl.loop(0, GROUPS)
-        def _(g):
+        blocks(n, ss, False)
+
+    def image(n):
+        i = n // 2
+        plane_wait(ss, 2, n)
+        row_wait(ss, 1, n)
+
+        @pl.loop(0, 2)
+        def _(e):
+            g = 2 * (n % 2) + e
             for p in range(PLANES):
                 for row in range(TOP, BOT, STEP):
                     aa[i, g, p, pl.ds(row - TOP, STEP), :] = stencil(ss, pw, i, g, p, row, 1.0, 0.0)
 
+        blocks(n, aa, True)
+
     line_slot = 2 * x + c
     lane16 = lax.broadcasted_iota(jnp.int32, (16, 128), 1)
 
     def gather_tiles():
-        def body(u, out):
+        out = jnp.zeros((16, 128), F32)
+        for u in range(16):
             tile = jnp.sum(gp[u], axis=1)
-            return jnp.where(lane16 == u, jnp.sum(tile, axis=1, keepdims=True), out)
-
-        return lax.fori_loop(0, 16, body, jnp.zeros((16, 128), F32))
+            out = jnp.where(lane16 == u, jnp.sum(tile, axis=1, keepdims=True), out)
+        return out
 
     rounds = ((line, 0, 8, line_slot), (z_peers, 8, NZ, z), (y_peers, 8 + NZ, NY, y))
 
@@ -252,40 +324,47 @@
 
     pot_wait = remote(pw, pw, p_send, p_recv, right)
 
-    @pl.loop(0, VPG + 1)
+    parts = 2 * VPG
+
+    @pl.loop(0, VPG)
+    def _(i):
+        for h in range(2):
+            a_wait(2 * i + h)
+            plane_start(xs, 0, 2 * i + h)
+
+        @pl.when(i == 0)
+        def _():
+            pot_wait.wait_recv()
+            for g in range(GROUPS):
+                remote(xy.at[g], xy.at[g], k_send.at[0], k_recv.at[g], right).wait_recv()
+
+        @pl.when(i < VPG - 1)
+        def _():
+            @pl.loop(0, 2)
+            def _(h):
+                first(2 * i + h)
+
+    @pl.loop(0, parts)
     def _(t):
-        @pl.when(t < VPG)
-        def _():
-            a_wait(t)
-            halo_start(xs, 0, t)
-
-        @pl.when(t == 0)
-        def _():
-            pot_wait.wait_recv()
-
-        @pl.when(t > 0)
-        def _():
-            second(t - 1)
-
-        @pl.when(t < VPG)
-        def _():
-            first(t)
+        @pl.when(jnp.logical_and(t >= parts - 4, t < parts - 2))
+        def _():
+            first(t + 2)
+
+        second(t)
 
     round_start(0, 0, gather_tiles())
-    image(0)
     round_start(0, 1, round_sum(0, 0))
-    image(1)
     round_start(0, 2, round_sum(0, 1))
-    image(2)
+
     gram = round_sum(0, 2)
 
     row16 = lax.broadcasted_iota(jnp.int32, (16, 128), 0)
     work = jnp.where(lane16 < 16, gram, jnp.where(lane16 - 16 == row16, 1.0, 0.0))
-    for j in range(16):
-        scale = 1.0 / jnp.sqrt(work[j:j + 1, j:j + 1])
-        pivot = work[j:j + 1, :] * scale
-        column = work[:, j:j + 1] * scale
-        work = jnp.where(row16 > j, work - column * pivot, jnp.where(row16 == j, pivot, work))
+    for j in range(15):
+        column = work[:, j:j + 1] * (1.0 / work[j:j + 1, j:j + 1])
+        work = work - jnp.where(row16 > j, column, 0.0) * work[j:j + 1, :]
+    pivots = jnp.sum(jnp.where(lane16 == row16, work, 0.0), axis=1, keepdims=True)
+    work = work * (1.0 / jnp.sqrt(pivots))
     inverse = jnp.where(lane16 < 16, pltpu.roll(work, 112, 1), 0.0)
     norm = jnp.sqrt(jnp.full((16, 128), PLANES * 64 * ROWS * NX * LANES, F32))
     mat[...] = inverse * norm
@@ -302,8 +381,8 @@
         keep = pltpu.make_async_copy(buf.at[i, g], dst, o_recv.at[w, i, x])
         return here, send, keep
 
-    def rotate(src, lift, buf, out, w):
-        @pl.loop(0, VPG * GROUPS)
+    def rotate(src, lift, buf, out, w, begin, end):
+        @pl.loop(begin * GROUPS, end * GROUPS)
         def _(n):
             i, g = n // GROUPS, n % GROUPS
             v = g * VPG + i
@@ -328,18 +407,24 @@
             def _():
                 send.start()
 
-    rotate(ss, 2, rr, rot_out, 0)
-    image(3)
-    rotate(aa, 0, ii, img_out, 1)
-
-    @pl.loop(0, VPG)
-    def _(i):
-        blocks(i, aa, True)
-
-    round_start(1, 0, gather_tiles())
-    round_start(1, 1, round_sum(1, 0))
+    @pl.loop(0, parts)
+    def _(t):
+        plane_start(ss, 2, t)
+        row_start(ss, 1, t)
+
+    rotate(ss, 2, rr, rot_out, 0, 0, VPG)
+
+    @pl.loop(0, parts)
+    def _(t):
+        image(t)
+
+    round_start(1, 1, gather_tiles())
+    rotate(aa, 0, ii, img_out, 1, 0, 1)
     round_start(1, 2, round_sum(1, 1))
-    curvature = round_sum(1, 2)
+    rotate(aa, 0, ii, img_out, 1, 1, 2)
+    round_start(1, 0, round_sum(1, 2))
+    rotate(aa, 0, ii, img_out, 1, 2, VPG)
+    curvature = round_sum(1, 0)
     half = lax.dot_general(inverse, curvature, NT, precision=HI, preferred_element_type=F32)
     half = jnp.concatenate([half, jnp.zeros((16, 112), F32)], axis=1)
     ritz_out[...] = lax.dot_general(half, inverse, NT, precision=HI, preferred_element_type=F32)
@@ -357,9 +442,21 @@
         def _():
             a_remote(i, 0).wait_send()
 
+    @pl.loop(0, parts)
+    def _(t):
         for s, buf in enumerate((xs, fs, ss)):
-            for copy in halo_copies(buf, s, i):
+            for copy in plane_copies(buf, s, t):
                 copy.wait_send()
+        for s in range(2):
+            for copy in row_copies(s, t):
+                copy.wait_send()
+
+    for d in (1, 2, 3):
+        k_remote(d).wait_send()
+
+    @pl.when(c != x_lo)
+    def _():
+        k_remote(0).wait_send()
 
     for w in range(2):
         for n in range(3):
@@ -391,28 +488,31 @@
     return tuple(pl.pallas_call(
         kernel,
         out_shape=(
-            jax.ShapeDtypeStruct(start_block.shape, F32),
-            jax.ShapeDtypeStruct(start_block.shape, F32),
+            pltpu.VMEM(start_block.shape, F32),
+            pltpu.VMEM(start_block.shape, F32),
             jax.ShapeDtypeStruct((16, 16), F32),
         ),
         in_specs=[any_space, any_space],
-        out_specs=(any_space, any_space, pl.BlockSpec(memory_space=pltpu.VMEM)),
+        out_specs=(pl.BlockSpec(memory_space=pltpu.VMEM), pl.BlockSpec(memory_space=pltpu.VMEM), pl.BlockSpec(memory_space=pltpu.VMEM)),
         scratch_shapes=[
             field, field, field, inner, inner, inner,
             pltpu.VMEM((PLANES, ROWS, LANES), F32),
-            pltpu.VMEM((3, VPG, 2, GROUPS, PLANES, LANES), F32),
-            pltpu.VMEM((3, VPG, 2, GROUPS, PLANES, LANES), F32),
+            pltpu.VMEM((NX - 1, VPG, PLANES, 16, LANES), F32),
+            pltpu.VMEM((NX, VPG, 2, PLANES, LANES), F32),
+            pltpu.VMEM((GROUPS, VPG, 2, PLANES, LANES), F32),
+            pltpu.VMEM((2, 2 * VPG, 2, 2, PLANES, LANES), F32),
+            pltpu.VMEM((2, 2 * VPG, 2, 2, PLANES, LANES), F32),
             pltpu.VMEM((16, 16, 8, 128), F32),
             pltpu.VMEM((2, 8 + NZ + NY, 16, 128), F32),
             pltpu.VMEM((16, 128), F32),
             pltpu.SMEM((16, 128), F32),
-            dma((VPG, 4)), dma((VPG, GROUPS)), dma, dma,
-            dma((3, VPG, 2)), dma((3, VPG, 2)), dma((3, VPG, 2)), dma((3, VPG, 2)),
+            dma((VPG, 4)), dma((VPG, GROUPS)), dma((NX - 1,)), dma((NX,)), dma((GROUPS,)), dma, dma,
+            dma((3, 2 * VPG, 2)), dma((3, 2 * VPG, 2)), dma((2, 2 * VPG, 2)), dma((2, 2 * VPG, 2)),
             dma((2, 8 + NZ + NY)), dma((2, 8 + NZ + NY)),
             dma((2, VPG, GROUPS)), dma((2, VPG, NX)), dma,
         ],
         compiler_params=pltpu.CompilerParams(
-            collective_id=0, has_side_effects=True, vmem_limit_bytes=56 * 2**20),
+            collective_id=0, has_side_effects=True, vmem_limit_bytes=48 * 2**20),
         name="filtered_subspace",
     )(start_block, potential))
 

time: 204 us -> 165 us (0.81)
  Pallas kernels: 197 us -> 160 us
  local copies, waits for them, and re-layouts: 6.25 us -> 3.93 us
    pallas_call x1, Pallas kernels: 197 us -> 160 us  [body(): pl.pallas_call(kernel, out_shape=(pltpu.VMEM(start_block.shape, F32), plt...]
    unnamed x7 -> x5, local copies, waits for them, and re-layouts: 6.25 us -> 3.93 us
where the time goes in v2:
time: 165 us
  Pallas kernels  160 us (97%)
  local copies, waits for them, and re-layouts  3.93 us (2%)
    pallas_call x1, Pallas kernels, body(): pl.pallas_call(kernel, out_shape=(pltpu.VMEM(start_block.shape, F32), plt...  160 us
    unnamed x5, local copies, waits for them, and re-layouts  3.93 us

profile of v2, /device:TPU:1, one launch (start us, length us, event | category | flops | bytes accessed | tf_op | source)
XLA Modules:
  0.0 165.1 jit_solution(5963820732500696020)
XLA Ops:
  0.6 160.5 %filtered_subspace.1 = (f32[4,4,192,256]{3,2,1,0:T(8,128)S(1)}, f32[4,4,192,256]{3,2,1,0:T(8,128)S(1)}, f32[16,16]{1,0:T(8,128)}) custom-call(f32[4,4,192,256]{3,2,1,0:T(8,128)} %start.1, f32[4,192,256]{2,1,0:T(8,128)} %pot.1), custom_call_target="tpu_custom_call" | custom-call | tf_op jit(solution)/shard_map/filtered_subspace/pallas_call | solution.py:488
  161.1 1.7 %copy.8 = f32[4,4,192,256]{3,2,1,0:T(8,128)} copy(f32[4,4,192,256]{3,2,1,0:T(8,128)S(1)} %get-tuple-element.3) | data formatting | bytes 6291456
  162.8 0.0 copy-start
  162.8 1.7 %copy.9 = f32[4,4,192,256]{3,2,1,0:T(8,128)} copy(f32[4,4,192,256]{3,2,1,0:T(8,128)S(1)} %get-tuple-element.4) | data formatting | bytes 6291456
  164.5 0.0 copy-done
  164.5 0.6 copy.10
Async XLA Ops:
  162.8 1.7 %copy-start = (f32[16,16]{1,0:T(8,128)S(1)}, f32[16,16]{1,0:T(8,128)}, u32[]{:S(2)}) copy-start(f32[16,16]{1,0:T(8,128)} %get-tuple-element.11) | copy-start | bytes 3076

commit v3 on v2

--- a/solution.py
+++ b/solution.py
@@ -17,6 +17,7 @@
 LANES = 256
 TOP, BOT = 8, 8 + ROWS
 STEP = 16
+AHEAD = 2
 NT = (((1,), (1,)), ((), ()))
 
 
@@ -44,9 +45,9 @@
 
 
 def kernel(start, pot, rot_out, img_out, ritz_out,
-           xs, fs, ss, aa, rr, ii, pw, edge, pack, xy, ysend, yrecv, gp, red, mat, inv_s,
+           xs, fs, ss, aa, rr, ii, pw, edge, pack, xy, ysend, yrecv, gp, red, mat, ps, sib, inv_s,
            a_send, a_recv, e_sem, k_send, k_recv, p_send, p_recv, h_send, h_recv, y_send, y_recv,
-           r_send, r_recv, o_send, o_recv, s_sem):
+           r_send, r_recv, o_send, o_recv, q_send, q_recv, t_send, t_recv, s_sem):
     x, y, z, c = place()
     x_lo = x % 2
     mine = lax.axis_index("vec")
@@ -258,10 +259,36 @@
                 for o in range(GROUPS):
                     gp[g * VPG + i, o * VPG + i] = accs[g * GROUPS + o]
 
+    def q_copy(i, j):
+        to_x, to_c = 2 * (j // 2) + c, j % 2
+        src = ss.at[i, :, 2 + PLANES - AHEAD + to_c, own_rows, :]
+        dst = ps.at[i, :, pl.ds(pl.multiple_of(ROWS * x, 8), ROWS), :]
+        here = jnp.logical_and(to_x == x, to_c == c)
+        send = remote(src, dst, q_send.at[i, j], q_recv.at[i, x], device(to_x, y, z, to_c))
+        return here, send, pltpu.make_async_copy(src, dst, q_recv.at[i, x])
+
+    def q_start(i):
+        for j in range(4):
+            here, send, keep = q_copy(i, j)
+
+            @pl.when(here)
+            def _():
+                keep.start()
+
+            @pl.when(jnp.logical_not(here))
+            def _():
+                send.start()
+
     def second(n):
         i = n // 2
         plane_wait(fs, 1, n)
         row_wait(fs, 0, n)
+
+        @pl.when(n == 2 * VPG - 1)
+        def _():
+            @pl.loop(0, VPG)
+            def _(t):
+                plane_start(ss, 2, t)
 
         @pl.loop(0, 2)
         def _(e):
@@ -272,6 +299,7 @@
                     ss[i, g, p + 2, rows, :] = (
                         stencil(fs, pw, i, g, p, row, 1.0, 3.0) - xs[i, g, p + 2, rows, :])
 
+        row_start(ss, 1, n)
         blocks(n, ss, False)
 
     def image(n):
@@ -352,7 +380,17 @@
 
         second(t)
 
+        @pl.when(t == 1)
+        def _():
+            q_start(0)
+
+        @pl.when(t == parts - 3)
+        def _():
+            q_start(1)
+
     round_start(0, 0, gather_tiles())
+    q_start(2)
+    q_start(3)
     round_start(0, 1, round_sum(0, 0))
     round_start(0, 2, round_sum(0, 1))
 
@@ -372,13 +410,16 @@
     to_smem.start()
     to_smem.wait()
 
+    sent = (PLANES - AHEAD, PLANES)
+
     def o_copy(out, buf, w, i, g):
         to_x = 2 * (g // 2) + c
         to_c = g % 2
-        dst = out.at[i, :, pl.ds(pl.multiple_of(ROWS * x, 8), ROWS), :]
+        src = buf.at[i, g, 0:sent[w]]
+        dst = out.at[i, 0:sent[w], pl.ds(pl.multiple_of(ROWS * x, 8), ROWS), :]
         here = jnp.logical_and(to_x == x, to_c == c)
-        send = remote(buf.at[i, g], dst, o_send.at[w, i, g], o_recv.at[w, i, x], device(to_x, y, z, to_c))
-        keep = pltpu.make_async_copy(buf.at[i, g], dst, o_recv.at[w, i, x])
+        send = remote(src, dst, o_send.at[w, i, g], o_recv.at[w, i, x], device(to_x, y, z, to_c))
+        keep = pltpu.make_async_copy(src, dst, o_recv.at[w, i, x])
         return here, send, keep
 
     def rotate(src, lift, buf, out, w, begin, end):
@@ -388,7 +429,7 @@
             v = g * VPG + i
             coef = [inv_s[v, u] for u in range(16)]
 
-            @pl.loop(0, PLANES)
+            @pl.loop(0, sent[w])
             def _(p):
                 for row in range(0, ROWS, STEP):
                     acc = None
@@ -407,12 +448,52 @@
             def _():
                 send.start()
 
-    @pl.loop(0, parts)
+    sibling = device(x, y, z, 1 - c)
+    my_plane = PLANES - AHEAD + c
+
+    def t_copy(i):
+        return remote(sib.at[i], rot_out.at[i, my_plane], t_send.at[i], t_recv.at[i], sibling)
+
+    def rotate_ahead(core, store):
+        @pl.loop(0, VPG)
+        def _(i):
+            v = (2 * (x // 2) + core) * VPG + i
+            coef = [inv_s[v, u] for u in range(16)]
+
+            @pl.loop(0, NX * ROWS // STEP)
+            def _(r):
+                rows = pl.ds(pl.multiple_of(r * STEP, STEP), STEP)
+                acc = None
+                for u in range(16):
+                    term = coef[u] * ps[u % VPG, u // VPG, rows, :]
+                    acc = term if acc is None else acc + term
+                store(i, rows, acc)
+
+    def to_sibling(i, rows, value):
+        sib[i, rows, :] = value
+
+    def to_output(i, rows, value):
+        rot_out[i, my_plane, rows, :] = value
+
+    @pl.loop(VPG, parts)
     def _(t):
         plane_start(ss, 2, t)
-        row_start(ss, 1, t)
 
     rotate(ss, 2, rr, rot_out, 0, 0, VPG)
+
+    @pl.loop(0, VPG)
+    def _(i):
+        for xx in range(NX):
+            dst = ps.at[i, :, pl.ds(ROWS * xx, ROWS), :]
+            remote(dst, dst, q_send.at[i, 0], q_recv.at[i, xx], right).wait_recv()
+
+    rotate_ahead(1 - c, to_sibling)
+
+    @pl.loop(0, VPG)
+    def _(i):
+        t_copy(i).start()
+
+    rotate_ahead(c, to_output)
 
     @pl.loop(0, parts)
     def _(t):
@@ -451,6 +532,18 @@
             for copy in row_copies(s, t):
                 copy.wait_send()
 
+    @pl.loop(0, VPG)
+    def _(i):
+        t_copy(i).wait_send()
+        theirs = rot_out.at[i, 2 * PLANES - 2 * AHEAD + 1 - my_plane]
+        remote(theirs, theirs, t_send.at[i], t_recv.at[i], sibling).wait_recv()
+        for j in range(4):
+            here, send, keep = q_copy(i, j)
+
+            @pl.when(jnp.logical_not(here))
+            def _():
+                send.wait_send()
+
     for d in (1, 2, 3):
         k_remote(d).wait_send()
 
@@ -476,7 +569,7 @@
         @pl.loop(0, VPG)
         def _(i):
             for xx in range(NX):
-                dst = out.at[i, :, pl.ds(ROWS * xx, ROWS), :]
+                dst = out.at[i, 0:sent[w], pl.ds(ROWS * xx, ROWS), :]
                 remote(dst, dst, o_send.at[w, i, 0], o_recv.at[w, i, xx], right).wait_recv()
 
 
@@ -505,11 +598,13 @@
             pltpu.VMEM((16, 16, 8, 128), F32),
             pltpu.VMEM((2, 8 + NZ + NY, 16, 128), F32),
             pltpu.VMEM((16, 128), F32),
+            pltpu.VMEM((VPG, GROUPS, NX * ROWS, LANES), F32),
+            pltpu.VMEM((VPG, NX * ROWS, LANES), F32),
             pltpu.SMEM((16, 128), F32),
             dma((VPG, 4)), dma((VPG, GROUPS)), dma((NX - 1,)), dma((NX,)), dma((GROUPS,)), dma, dma,
             dma((3, 2 * VPG, 2)), dma((3, 2 * VPG, 2)), dma((2, 2 * VPG, 2)), dma((2, 2 * VPG, 2)),
             dma((2, 8 + NZ + NY)), dma((2, 8 + NZ + NY)),
-            dma((2, VPG, GROUPS)), dma((2, VPG, NX)), dma,
+            dma((2, VPG, GROUPS)), dma((2, VPG, NX)), dma((VPG, 4)), dma((VPG, NX)), dma((VPG,)), dma((VPG,)), dma,
         ],
         compiler_params=pltpu.CompilerParams(
             collective_id=0, has_side_effects=True, vmem_limit_bytes=48 * 2**20),

time: 165 us -> 154 us (0.933)
  Pallas kernels: 160 us -> 149 us
    pallas_call x1, Pallas kernels: 160 us -> 149 us  [body(): pl.pallas_call(kernel, out_shape=(pltpu.VMEM(start_block.shape, F32), plt...]
where the time goes in v3:
time: 154 us
  Pallas kernels  149 us (97%)
  local copies, waits for them, and re-layouts  3.93 us (3%)
    pallas_call x1, Pallas kernels, body(): pl.pallas_call(kernel, out_shape=(pltpu.VMEM(start_block.shape, F32), plt...  149 us
    unnamed x5, local copies, waits for them, and re-layouts  3.93 us

profile of v3, /device:TPU:1, one launch (start us, length us, event | category | flops | bytes accessed | tf_op | source)
XLA Modules:
  0.0 153.5 jit_solution(2431878987501948048)
XLA Ops:
  0.6 149.0 %filtered_subspace.1 = (f32[4,4,192,256]{3,2,1,0:T(8,128)S(1)}, f32[4,4,192,256]{3,2,1,0:T(8,128)S(1)}, f32[16,16]{1,0:T(8,128)}) custom-call(f32[4,4,192,256]{3,2,1,0:T(8,128)} %start.1, f32[4,192,256]{2,1,0:T(8,128)} %pot.1), custom_call_target="tpu_custom_call" | custom-call | tf_op jit(solution)/shard_map/filtered_subspace/pallas_call | solution.py:581
  149.6 1.7 %copy.8 = f32[4,4,192,256]{3,2,1,0:T(8,128)} copy(f32[4,4,192,256]{3,2,1,0:T(8,128)S(1)} %get-tuple-element.3) | data formatting | bytes 6291456
  151.3 0.0 copy-start
  151.3 1.7 %copy.9 = f32[4,4,192,256]{3,2,1,0:T(8,128)} copy(f32[4,4,192,256]{3,2,1,0:T(8,128)S(1)} %get-tuple-element.4) | data formatting | bytes 6291456
  152.9 0.0 copy-done
  152.9 0.6 copy.10
Async XLA Ops:
  151.3 1.7 %copy-start = (f32[16,16]{1,0:T(8,128)S(1)}, f32[16,16]{1,0:T(8,128)}, u32[]{:S(2)}) copy-start(f32[16,16]{1,0:T(8,128)} %get-tuple-element.11) | copy-start | bytes 3076

commit v4 on v3

--- a/solution.py
+++ b/solution.py
@@ -374,19 +374,20 @@
 
     @pl.loop(0, parts)
     def _(t):
-        @pl.when(jnp.logical_and(t >= parts - 4, t < parts - 2))
+        @pl.when(t == parts - 4)
         def _():
             first(t + 2)
 
+        @pl.when(t == parts - 3)
+        def _():
+            first(t + 2)
+            q_start(1)
+
         second(t)
 
         @pl.when(t == 1)
         def _():
             q_start(0)
-
-        @pl.when(t == parts - 3)
-        def _():
-            q_start(1)
 
     round_start(0, 0, gather_tiles())
     q_start(2)
@@ -583,7 +584,7 @@
         out_shape=(
             pltpu.VMEM(start_block.shape, F32),
             pltpu.VMEM(start_block.shape, F32),
-            jax.ShapeDtypeStruct((16, 16), F32),
+            pltpu.VMEM((16, 16), F32),
         ),
         in_specs=[any_space, any_space],
         out_specs=(pl.BlockSpec(memory_space=pltpu.VMEM), pl.BlockSpec(memory_space=pltpu.VMEM), pl.BlockSpec(memory_space=pltpu.VMEM)),

time: 154 us -> 152 us (0.987)
  Pallas kernels: 149 us -> 147 us
    pallas_call x1, Pallas kernels: 149 us -> 147 us  [body(): pl.pallas_call(kernel, out_shape=(pltpu.VMEM(start_block.shape, F32), plt...]
    unnamed x5 -> x3, local copies, waits for them, and re-layouts: 3.93 us -> 3.93 us
where the time goes in v4:
time: 152 us; the launch traced here: 151 us
  Pallas kernels  147 us (97%)
  local copies, waits for them, and re-layouts  3.93 us (3%)
    pallas_call x1, Pallas kernels, body(): pl.pallas_call(kernel, out_shape=(pltpu.VMEM(start_block.shape, F32), plt...  147 us
    unnamed x3, local copies, waits for them, and re-layouts  3.93 us

profile of v4, /device:TPU:1, one launch (start us, length us, event | category | flops | bytes accessed | tf_op | source)
XLA Modules:
  0.0 151.2 jit_solution(4666977612678091189)
XLA Ops:
  0.6 146.6 %filtered_subspace.1 = (f32[4,4,192,256]{3,2,1,0:T(8,128)S(1)}, f32[4,4,192,256]{3,2,1,0:T(8,128)S(1)}, f32[16,16]{1,0:T(8,128)S(1)}) custom-call(f32[4,4,192,256]{3,2,1,0:T(8,128)} %start.1, f32[4,192,256]{2,1,0:T(8,128)} %pot.1), custom_call_target="tpu_custom_call" | custom-call | tf_op jit(solution)/shard_map/filtered_subspace/pallas_call | solution.py:582
  147.3 1.7 %copy.8 = f32[4,4,192,256]{3,2,1,0:T(8,128)} copy(f32[4,4,192,256]{3,2,1,0:T(8,128)S(1)} %get-tuple-element.3) | data formatting | bytes 6291456
  149.0 0.6 copy.10
  149.6 1.7 %copy.9 = f32[4,4,192,256]{3,2,1,0:T(8,128)} copy(f32[4,4,192,256]{3,2,1,0:T(8,128)S(1)} %get-tuple-element.4) | data formatting | bytes 6291456

commit v5 on v4

--- a/solution.py
+++ b/solution.py
@@ -482,6 +482,12 @@
 
     rotate(ss, 2, rr, rot_out, 0, 0, VPG)
 
+    @pl.loop(0, parts)
+    def _(t):
+        image(t)
+
+    rotate(aa, 0, ii, img_out, 1, 0, 1)
+    round_start(1, 1, gather_tiles())
     @pl.loop(0, VPG)
     def _(i):
         for xx in range(NX):
@@ -496,12 +502,6 @@
 
     rotate_ahead(c, to_output)
 
-    @pl.loop(0, parts)
-    def _(t):
-        image(t)
-
-    round_start(1, 1, gather_tiles())
-    rotate(aa, 0, ii, img_out, 1, 0, 1)
     round_start(1, 2, round_sum(1, 1))
     rotate(aa, 0, ii, img_out, 1, 1, 2)
     round_start(1, 0, round_sum(1, 2))

time: 152 us -> 151 us (level)
  no operation moved by 1% of the time
where the time goes in v5:
time: 151 us
  Pallas kernels  147 us (97%)
  local copies, waits for them, and re-layouts  3.93 us (3%)
    pallas_call x1, Pallas kernels, body(): pl.pallas_call(kernel, out_shape=(pltpu.VMEM(start_block.shape, F32), plt...  147 us
    unnamed x3, local copies, waits for them, and re-layouts  3.93 us

profile of v5, /device:TPU:1, one launch (start us, length us, event | category | flops | bytes accessed | tf_op | source)
XLA Modules:
  0.0 151.2 jit_solution(14492125394060559532)
XLA Ops:
  0.6 146.6 %filtered_subspace.1 = (f32[4,4,192,256]{3,2,1,0:T(8,128)S(1)}, f32[4,4,192,256]{3,2,1,0:T(8,128)S(1)}, f32[16,16]{1,0:T(8,128)S(1)}) custom-call(f32[4,4,192,256]{3,2,1,0:T(8,128)} %start.1, f32[4,192,256]{2,1,0:T(8,128)} %pot.1), custom_call_target="tpu_custom_call" | custom-call | tf_op jit(solution)/shard_map/filtered_subspace/pallas_call | solution.py:582
  147.3 1.7 %copy.8 = f32[4,4,192,256]{3,2,1,0:T(8,128)} copy(f32[4,4,192,256]{3,2,1,0:T(8,128)S(1)} %get-tuple-element.3) | data formatting | bytes 6291456
  149.0 0.6 copy.10
  149.6 1.7 %copy.9 = f32[4,4,192,256]{3,2,1,0:T(8,128)} copy(f32[4,4,192,256]{3,2,1,0:T(8,128)S(1)} %get-tuple-element.4) | data formatting | bytes 6291456
